TPU v7x, 32 devices: a whole 2x2x4 slice. The times are simulated.
32 devices in a mesh: fsdp: 4 (over z), ctx: 4 (over y, core), tp: 2 (over x).
Axes of the slice: x: 2, y: 2, z: 4, core: 2. Of those that a mesh axis runs over, the one named last changes fastest.
Arguments:
- block_input: bfloat16 [4, 1024, 1024], P('fsdp', 'ctx'), may hold values from -6 to 6
- input_gain: float32 [1024], replicated, may hold values from 0.5 to 1.5
- gate_proj: bfloat16 [1024, 2048], P('fsdp', 'tp'), may hold values from -0.1875 to 0.1875
- x_proj: bfloat16 [1024, 2048], P('fsdp', 'tp'), may hold values from -0.1875 to 0.1875
- bc_proj: bfloat16 [1024, 256], P('fsdp'), may hold values from -0.1875 to 0.1875
- dt_proj: bfloat16 [1024, 32], P('fsdp', 'tp'), may hold values from -0.1875 to 0.1875
- x_conv: float32 [4, 2048], P(None, 'tp'), may hold values from -3 to 3
- bc_conv: float32 [4, 256], replicated, may hold values from -3 to 3
- dt_bias: float32 [32], P('tp'), may hold values from -2 to 1
- a_log: float32 [32], P('tp'), may hold values from -11 to -2
- skip_gain: float32 [32], P('tp'), may hold values from 0.5 to 1.5
- gated_gain: float32 [2048], P('tp'), may hold values from 0.5 to 1.5
- out_proj: bfloat16 [2048, 1024], P('tp', 'fsdp'), may hold values from -0.125 to 0.125
- cotangent: bfloat16 [4, 1024, 1024], P('fsdp', 'ctx'), may hold values from -6 to 6
Outputs:
- block_output: bfloat16 [4, 1024, 1024], P('fsdp', 'ctx')
- input_grad: float32 [4, 1024, 1024], P('fsdp', 'ctx')
- grad_input_gain: float32 [1024], replicated
- grad_gate_proj: float32 [1024, 2048], P('fsdp', 'tp')
- grad_x_proj: float32 [1024, 2048], P('fsdp', 'tp')
- grad_bc_proj: float32 [1024, 256], P('fsdp')
- grad_dt_proj: float32 [1024, 32], P('fsdp', 'tp')
- grad_x_conv: float32 [4, 2048], P(None, 'tp')
- grad_bc_conv: float32 [4, 256], replicated
- grad_dt_bias: float32 [32], P('tp')
- grad_a_log: float32 [32], P('tp')
- grad_skip_gain: float32 [32], P('tp')
- grad_gated_gain: float32 [2048], P('tp')
- grad_out_proj: float32 [2048, 1024], P('tp', 'fsdp')
All inputs are finite; a program needn't handle non-finite values.
Results may differ from a plain program's by a relative error of at most 0.0098.
Values may be sent and summed in bfloat16 or wider, within the bound.
No kernel may reach another device: no remote copies, remote signals or barrier semaphores. Data moves between devices by JAX's collectives and lax.ppermute only.
A program may use at most 128 MiB of HBM per device.

v0:
```python
import jax
import jax.numpy as jnp
from jax import lax
from jax.sharding import PartitionSpec as P

EPSILON = 1e-05
FINE = lax.Precision.HIGHEST


def from_behind(block, axis, distance):
    devices = range(lax.axis_size(axis))
    route = [(i - distance, i) for i in devices if i - distance in devices]
    return lax.ppermute(block, axis, route)


def carried_in(part, axis, combine, identity, reverse):
    count = lax.axis_size(axis)
    place = lax.axis_index(axis)
    ahead = count - 1 - place if reverse else place
    gathered = jax.tree.map(lambda a: lax.all_gather(a, axis), part)
    state = jax.tree.map(lambda a, e: jnp.zeros_like(a) + jnp.asarray(e, a.dtype), part, identity)

    def one(lap, state):
        source = count - 1 - lap if reverse else lap
        return combine(
            state, jax.tree.map(lambda a: lax.dynamic_index_in_dim(a, source, 0, False), gathered)
        )

    return lax.fori_loop(0, ahead, one, state)


def combine_states(earlier, later):
    return (earlier[0] * later[0], earlier[1] * later[0][:, :, None, None] + later[1])


def silu_slope(values):
    sigmoid_value = jax.nn.sigmoid(values)
    return sigmoid_value * (1.0 + values * (1.0 - sigmoid_value))


def block_local(x_heads, b_rows, c_rows, step_size, log_decay):
    cumulative = jnp.cumsum(log_decay, axis=2)
    log_gaps = cumulative[:, :, :, None] - cumulative[:, :, None, :]
    length = log_decay.shape[2]
    causal = jnp.tril(jnp.ones((length, length), jnp.bool_))
    decays = jnp.where(causal, jnp.exp(jnp.where(causal, log_gaps, 0.0)), 0.0)
    scores = jnp.einsum("btn,bsn->bts", c_rows, b_rows, precision=FINE)
    weights = decays * scores[:, None, :, :] * step_size[:, :, None, :]
    within = jnp.einsum("bhts,bshp->bthp", weights, x_heads, precision=FINE)
    tail_decay = jnp.exp(cumulative[:, :, -1:] - cumulative) * step_size
    summary = jnp.einsum("bhs,bshp,bsn->bhpn", tail_decay, x_heads, b_rows, precision=FINE)
    return (within, summary, jnp.exp(cumulative[:, :, -1]))


def block_carry(c_rows, log_decay, state_in):
    cumulative = jnp.cumsum(log_decay, axis=2)
    carried = jnp.einsum("btn,bhpn->bthp", c_rows, state_in, precision=FINE)
    return jnp.exp(cumulative).transpose(0, 2, 1)[:, :, :, None] * carried


def back_product(grad_low, weight):
    return lax.dot_general(
        grad_low, weight, (((1,), (1,)), ((), ())), preferred_element_type=jnp.float32
    )


def on_device(
    block_input,
    input_gain,
    gate_proj,
    x_proj,
    bc_proj,
    dt_proj,
    x_conv,
    bc_conv,
    dt_bias,
    a_log,
    skip_gain,
    gated_gain,
    out_proj,
    cotangent,
):
    seqs_here, length, model_width = block_input.shape
    row_count = seqs_here * length
    inner_here = gate_proj.shape[1]
    heads_here = dt_proj.shape[1]
    head_size = inner_here // heads_here
    state_size = bc_proj.shape[1] // 2
    tap_count = x_conv.shape[0]
    full_inner = inner_here * lax.axis_size("tp")
    full_gate, full_x, full_bc, full_dt, full_out = (
        lax.all_gather(gate_proj, "fsdp", axis=0, tiled=True),
        lax.all_gather(x_proj, "fsdp", axis=0, tiled=True),
        lax.all_gather(bc_proj, "fsdp", axis=0, tiled=True),
        lax.all_gather(dt_proj, "fsdp", axis=0, tiled=True),
        lax.all_gather(out_proj, "fsdp", axis=1, tiled=True),
    )
    residual = block_input.astype(jnp.float32)
    in_scale = lax.rsqrt(jnp.mean(residual * residual, axis=-1, keepdims=True) + EPSILON)
    normed_low = (
        (residual * in_scale * input_gain).astype(jnp.bfloat16).reshape(row_count, model_width)
    )
    gate_input = jnp.dot(normed_low, full_gate, preferred_element_type=jnp.float32).reshape(
        seqs_here, length, inner_here
    )
    x_input = jnp.dot(normed_low, full_x, preferred_element_type=jnp.float32).reshape(
        seqs_here, length, inner_here
    )
    bc_input = jnp.dot(normed_low, full_bc, preferred_element_type=jnp.float32).reshape(
        seqs_here, length, 2 * state_size
    )
    dt_input = jnp.dot(normed_low, full_dt, preferred_element_type=jnp.float32).reshape(
        seqs_here, length, heads_here
    )
    conv_input = jnp.concatenate([x_input, bc_input], axis=-1)
    conv_taps = jnp.concatenate([x_conv, bc_conv], axis=-1)
    edge_rows = from_behind(conv_input[:, length - tap_count + 1 :, :], "ctx", 1)
    padded = jnp.concatenate([edge_rows, conv_input], axis=1)
    conv_out = jnp.zeros_like(conv_input)
    for offset in range(tap_count):
        conv_out = conv_out + conv_taps[offset] * padded[:, offset : offset + length, :]
    activated = jax.nn.silu(conv_out)
    x_heads = activated[:, :, :inner_here].reshape(seqs_here, length, heads_here, head_size)
    b_rows = activated[:, :, inner_here : inner_here + state_size]
    c_rows = activated[:, :, inner_here + state_size :]
    pre_step = dt_input.transpose(0, 2, 1) + dt_bias[None, :, None]
    step_size = jax.nn.softplus(pre_step)
    decay_rates = jnp.exp(a_log)[None, :, None]
    log_decay = -decay_rates * step_size
    (within, summary, total_decay), local_back = jax.vjp(
        block_local, x_heads, b_rows, c_rows, step_size, log_decay
    )
    identity = (jnp.ones_like(total_decay), jnp.zeros_like(summary))
    state_in = carried_in((total_decay, summary), "ctx", combine_states, identity, False)[1]
    carried, carry_back = jax.vjp(block_carry, c_rows, log_decay, state_in)
    mixed_heads = within + carried + skip_gain[None, None, :, None] * x_heads
    mixed_flat = mixed_heads.reshape(seqs_here, length, inner_here)
    gate_act = jax.nn.silu(gate_input)
    gated_rows = mixed_flat * gate_act
    square_sum = lax.psum(jnp.sum(gated_rows * gated_rows, axis=-1), "tp")
    out_scale = lax.rsqrt(square_sum / full_inner + EPSILON)[:, :, None]
    normed_out = (
        (gated_rows * out_scale * gated_gain).astype(jnp.bfloat16).reshape(row_count, inner_here)
    )
    branch_sum = lax.psum(jnp.dot(normed_out, full_out, preferred_element_type=jnp.float32), "tp")
    block_output = (residual + branch_sum.reshape(seqs_here, length, model_width)).astype(
        jnp.bfloat16
    )
    cot_rows = cotangent.reshape(row_count, model_width)
    grad_out_w = lax.dot_general(
        normed_out, cot_rows, (((0,), (0,)), ((), ())), preferred_element_type=jnp.float32
    )
    d_normed_low = back_product(cot_rows, full_out).astype(jnp.bfloat16)
    d_normed_out = d_normed_low.astype(jnp.float32).reshape(seqs_here, length, inner_here)
    grad_gated_gain = jnp.sum(d_normed_out * gated_rows * out_scale, axis=(0, 1))
    cross_sum = lax.psum(jnp.sum(d_normed_out * gated_gain * gated_rows, axis=-1), "tp")
    d_gated = (
        out_scale * gated_gain * d_normed_out
        - gated_rows * (out_scale**3 / full_inner) * cross_sum[:, :, None]
    )
    d_mixed = (d_gated * gate_act).reshape(seqs_here, length, heads_here, head_size)
    d_gate_low = (
        (d_gated * mixed_flat * silu_slope(gate_input))
        .astype(jnp.bfloat16)
        .reshape(row_count, inner_here)
    )
    grad_skip_gain = jnp.sum(d_mixed * x_heads, axis=(0, 1, 3))
    d_c_carry, d_decay_carry, state_grad = carry_back(d_mixed)
    later_grad = carried_in((total_decay, state_grad), "ctx", combine_states, identity, True)[1]
    d_total = jnp.sum(later_grad * state_in, axis=(2, 3))
    d_x_heads, d_b_rows, d_c_rows, d_step, d_log_decay = local_back((d_mixed, later_grad, d_total))
    d_x_heads = d_x_heads + skip_gain[None, None, :, None] * d_mixed
    d_c_rows = d_c_rows + d_c_carry
    d_log_decay = d_log_decay + d_decay_carry
    grad_a_log = jnp.sum(d_log_decay * log_decay, axis=(0, 2))
    d_pre = (d_step - decay_rates * d_log_decay) * jax.nn.sigmoid(pre_step)
    grad_dt_bias = jnp.sum(d_pre, axis=(0, 2))
    d_dt_low = d_pre.transpose(0, 2, 1).astype(jnp.bfloat16).reshape(row_count, heads_here)
    d_activated = jnp.concatenate(
        [d_x_heads.reshape(seqs_here, length, inner_here), d_b_rows, d_c_rows], axis=-1
    )
    d_conv_out = d_activated * silu_slope(conv_out)
    d_padded = jnp.zeros_like(padded)
    tap_grads = []
    for offset in range(tap_count):
        tap_grads.append(jnp.sum(d_conv_out * padded[:, offset : offset + length, :], axis=(0, 1)))
        d_padded = d_padded.at[:, offset : offset + length, :].add(conv_taps[offset] * d_conv_out)
    grad_taps = jnp.stack(tap_grads)
    edge_grad = from_behind(d_padded[:, : tap_count - 1, :], "ctx", -1)
    d_conv_input = d_padded[:, tap_count - 1 :, :] + jnp.pad(
        edge_grad, ((0, 0), (length - tap_count + 1, 0), (0, 0))
    )
    d_x_low = d_conv_input[:, :, :inner_here].astype(jnp.bfloat16).reshape(row_count, inner_here)
    partial_normed = (
        back_product(d_gate_low, full_gate)
        + back_product(d_x_low, full_x)
        + back_product(d_dt_low, full_dt)
    )
    summed_normed, summed_bc, grad_bc_conv = lax.psum(
        (
            partial_normed,
            d_conv_input[:, :, inner_here:].reshape(row_count, 2 * state_size),
            grad_taps[:, inner_here:],
        ),
        "tp",
    )
    d_bc_low = summed_bc.astype(jnp.bfloat16)
    d_normed = (summed_normed + back_product(d_bc_low, full_bc)).reshape(
        seqs_here, length, model_width
    )

    def weight_grad(grad_low):
        return lax.dot_general(
            normed_low, grad_low, (((0,), (0,)), ((), ())), preferred_element_type=jnp.float32
        )

    weight_grads = (
        weight_grad(d_gate_low),
        weight_grad(d_x_low),
        weight_grad(d_bc_low),
        weight_grad(d_dt_low),
        grad_out_w,
    )
    grad_input_gain = jnp.sum(d_normed * residual * in_scale, axis=(0, 1))
    d_scaled = d_normed * input_gain
    input_grad = (
        cotangent.astype(jnp.float32)
        + in_scale * d_scaled
        - residual
        * (in_scale**3 / model_width)
        * jnp.sum(d_scaled * residual, axis=-1, keepdims=True)
    )
    sectioned = (
        lax.psum_scatter(weight_grads[0], "fsdp", scatter_dimension=0, tiled=True),
        lax.psum_scatter(weight_grads[1], "fsdp", scatter_dimension=0, tiled=True),
        lax.psum_scatter(weight_grads[2], "fsdp", scatter_dimension=0, tiled=True),
        lax.psum_scatter(weight_grads[3], "fsdp", scatter_dimension=0, tiled=True),
        lax.psum_scatter(weight_grads[4], "fsdp", scatter_dimension=1, tiled=True),
    )
    owned_rows = (
        lax.psum_scatter(sectioned[0], "ctx", scatter_dimension=0, tiled=True),
        lax.psum_scatter(sectioned[1], "ctx", scatter_dimension=0, tiled=True),
        lax.psum_scatter(sectioned[2], "ctx", scatter_dimension=0, tiled=True),
        lax.psum_scatter(sectioned[3], "ctx", scatter_dimension=0, tiled=True),
        lax.psum_scatter(sectioned[4], "ctx", scatter_dimension=1, tiled=True),
    )
    grad_gate_proj, grad_x_proj, grad_bc_proj, grad_dt_proj, grad_out_proj = (
        lax.all_gather(owned_rows[0], "ctx", axis=0, tiled=True),
        lax.all_gather(owned_rows[1], "ctx", axis=0, tiled=True),
        lax.all_gather(owned_rows[2], "ctx", axis=0, tiled=True),
        lax.all_gather(owned_rows[3], "ctx", axis=0, tiled=True),
        lax.all_gather(owned_rows[4], "ctx", axis=1, tiled=True),
    )
    small_totals = lax.psum(
        (
            grad_input_gain,
            grad_taps[:, :inner_here],
            grad_bc_conv,
            grad_dt_bias,
            grad_a_log,
            grad_skip_gain,
            grad_gated_gain,
        ),
        ("fsdp", "ctx"),
    )
    return (
        block_output,
        input_grad,
        small_totals[0],
        grad_gate_proj,
        grad_x_proj,
        grad_bc_proj,
        grad_dt_proj,
        small_totals[1],
        small_totals[2],
        small_totals[3],
        small_totals[4],
        small_totals[5],
        small_totals[6],
        grad_out_proj,
    )


def solution(mesh):
    in_specs = (
        P("fsdp", "ctx", None),
        P(),
        P("fsdp", "tp"),
        P("fsdp", "tp"),
        P("fsdp", None),
        P("fsdp", "tp"),
        P(None, "tp"),
        P(),
        P("tp"),
        P("tp"),
        P("tp"),
        P("tp"),
        P("tp", "fsdp"),
        P("fsdp", "ctx", None),
    )
    out_specs = (
        P("fsdp", "ctx", None),
        P("fsdp", "ctx", None),
        P(),
        P("fsdp", "tp"),
        P("fsdp", "tp"),
        P("fsdp", None),
        P("fsdp", "tp"),
        P(None, "tp"),
        P(),
        P("tp"),
        P("tp"),
        P("tp"),
        P("tp"),
        P("tp", "fsdp"),
    )
    return jax.shard_map(
        on_device, mesh=mesh, in_specs=in_specs, out_specs=out_specs, check_vma=False
    )
```

profile of v0, /device:TPU:0, one launch (start us, length us, event | category | flops | bytes accessed | tf_op | source)
XLA Modules:
  0.0 786.6 jit_solution(12926951627118034505)
XLA Ops:
  8.0 15.0 %all_gather.50 = bf16[1024,16]{0,1:T(8,128)(2,1)S(1)} all-gather(bf16[256,16]{0,1:T(8,128)(2,1)} %param.31), channel_id=1, replica_groups=mesh['fsdp'=4,'ctx'=4,'tp'=2] {'fsdp'}, dimensions={0}, use_global_device_ids=true | all-gather | bytes 40960 | tf_op jit(solution)/shard_map/all_gather | solution.py:95
  29.3 22.7 %all_gather.49 = bf16[1024,256]{1,0:T(8,128)(2,1)S(1)} all-gather(bf16[256,256]{1,0:T(8,128)(2,1)S(1)} %copy-done.44), channel_id=1, replica_groups=mesh['fsdp'=4,'ctx'=4,'tp'=2] {'fsdp'}, dimensions={0}, use_global_device_ids=true | all-gather | bytes 655360 | tf_op jit(solution)/shard_map/all_gather | solution.py:94
  54.0 12.6 %all-gather.13.cloned.1.call-done = bf16[1024,1024]{1,0:T(8,128)(2,1)} async-done(((bf16[256,1024]{1,0:T(8,128)(2,1)}), bf16[1024,1024]{1,0:T(8,128)(2,1)}) %all-gather.13.cloned.1.call-update) | async-done | bytes 2097168 | tf_op jit(solution)/shard_map/all_gather | solution.py:93
  77.2 3.0 fusion.62
  83.0 7.0 all-gather
  91.1 2.6 copy.207
  96.4 7.8 all-gather.25.cloned.1.call-done
  106.3 6.0 fusion.36
  112.3 2.6 copy.205
  114.9 36.8 %all-gather.15.cloned.1.call-done = bf16[1024,1024]{1,0:T(8,128)(2,1)} async-done(((bf16[256,1024]{1,0:T(8,128)(2,1)}), bf16[1024,1024]{1,0:T(8,128)(2,1)}) %all-gather.15.cloned.1.call-update) | async-done | bytes 2097168 | tf_op jit(solution)/shard_map/all_gather | solution.py:92
  151.7 3.7 multiply_reduce_fusion.8
  155.4 4.9 psum.91
  160.3 37.8 %all-gather.17.cloned.1.call-done = bf16[1024,1024]{1,0:T(8,128)(2,1)} async-done(((bf16[1024,256]{1,0:T(8,128)(2,1)}), bf16[1024,1024]{1,0:T(8,128)(2,1)}) %all-gather.17.cloned.1.call-update) | async-done | bytes 2097168 | tf_op jit(solution)/shard_map/all_gather | solution.py:96
  198.2 4.0 fusion.49
  202.2 5.4 psum.93
  207.6 2.9 fusion.59
  212.6 2.6 copy.208
  215.3 3.0 fusion.88
  221.5 2.8 fusion.121
  224.3 3.9 fusion.68
  228.3 2.6 copy.211
  231.0 8.6 %fusion.8 = (f32[16,256]{1,0:T(8,128)}, f32[16,256]{1,0:T(8,128)}, f32[16,256]{1,0:T(8,128)}, f32[256,256]{1,0:T(8,128)S(1)}) fusion(f32[16,256]{1,0:T(8,128)S(1)} %copy-done.57, f32[256,256]{1,0:T(8,128)} %fusion.92, f32[16,256]{1,0:T(8,128)S(1)} %copy-done.59, pred[256,256]{1,0:T(8,128)(4,1)} %iota_compare_fusion, f32[16,64,256]{2,1,0:T(8,128)} %bitcast.308, ...), kind=kOutput, calls=%fused_computation.20 | convolution fusion | flops 820957184 | bytes 2768896 | tf_op jit(solution)/shard_map/transpose(jvp(bhts,bshp->bthp))/dot_general | solution.py:49
  244.2 6.0 while.31
  252.7 4.9 fusion.30
  257.6 2.5 copy.216
  260.2 3.1 fusion.42
  263.3 2.6 multiply_reduce_fusion.5
  268.7 4.5 scatter-add.11
  273.2 2.6 slice_add_fusion.1
  275.8 4.4 scatter-add.14
  286.6 2.8 fusion.77
  300.4 12.9 %all-reduce.11 = (bf16[256,256]{1,0:T(8,128)(2,1)S(1)}, f32[4,256]{1,0:T(4,128)}) all-reduce(f32[256,256]{1,0:T(8,128)S(1)} %slice_bitcast_fusion, f32[4,256]{1,0:T(4,128)S(1)} %pad_maximum_fusion.2), channel_id=1, replica_groups=mesh['fsdp'=4,'ctx'=4,'tp'=2] {'tp'}, use_global_device_ids=true, to_apply=%region_24.25 | all-reduce | flops 66560 | bytes 401408 | tf_op jit(solution)/shard_map/psum | solution.py:199
  314.8 3.4 reduce-scatter.15.cloned.1.call-done
  318.3 79.6 %reduce-scatter.29.cloned.1.call-done = f32[1024,256]{1,0:T(8,128)} async-done(((f32[1024,1024]{1,0:T(8,128)}), f32[1024,256]{1,0:T(8,128)}) %reduce-scatter.29.cloned.1.call-update) | async-done | bytes 1048592 | tf_op jit(solution)/shard_map/reduce_scatter | solution.py:238
  400.6 77.0 %reduce-scatter.19.cloned.1.call-done = f32[256,1024]{1,0:T(8,128)} async-done(((f32[1024,1024]{1,0:T(8,128)}), f32[256,1024]{1,0:T(8,128)}) %reduce-scatter.19.cloned.1.call-update) | async-done | bytes 1048592 | tf_op jit(solution)/shard_map/reduce_scatter | solution.py:235
  477.6 3.5 convolution_bitcast_fusion
  483.5 16.5 %reduce-scatter.27.cloned.1.call-done = f32[256,16]{0,1:T(8,128)} async-done(((f32[1024,16]{0,1:T(8,128)}), f32[256,16]{0,1:T(8,128)}) %reduce-scatter.27.cloned.1.call-update) | async-done | bytes 16400 | tf_op jit(solution)/shard_map/reduce_scatter | solution.py:237
  502.9 25.2 %reduce-scatter.23.cloned.1.call-done = f32[256,256]{1,0:T(8,128)} async-done(((f32[1024,256]{1,0:T(8,128)}), f32[256,256]{1,0:T(8,128)}) %reduce-scatter.23.cloned.1.call-update) | async-done | bytes 262160 | tf_op jit(solution)/shard_map/reduce_scatter | solution.py:236
  528.2 26.2 %reduce-scatter.17.cloned.1.call-done = f32[64,1024]{1,0:T(8,128)} async-done(((f32[256,1024]{1,0:T(8,128)}), f32[64,1024]{1,0:T(8,128)}) %reduce-scatter.17.cloned.1.call-update) | async-done | bytes 262160 | tf_op jit(solution)/shard_map/reduce_scatter | solution.py:241
  554.4 27.2 %reduce-scatter.33.cloned.1.call-done = f32[64,1024]{1,0:T(8,128)} async-done(((f32[256,1024]{1,0:T(8,128)}), f32[64,1024]{1,0:T(8,128)}) %reduce-scatter.33.cloned.1.call-update) | async-done | bytes 262160
  581.7 27.6 %reduce-scatter.21.cloned.1.call-done = f32[64,1024]{1,0:T(8,128)} async-done(((f32[256,1024]{1,0:T(8,128)}), f32[64,1024]{1,0:T(8,128)}) %reduce-scatter.21.cloned.1.call-update) | async-done | bytes 262160 | tf_op jit(solution)/shard_map/reduce_scatter | solution.py:242
  609.5 22.1 %reduce-scatter.31.cloned.1.call-done = f32[64,16]{1,0:T(8,128)} async-done(((f32[256,16]{1,0:T(8,128)}), f32[64,16]{1,0:T(8,128)}) %reduce-scatter.31.cloned.1.call-update) | async-done | bytes 4112
  632.5 5.2 all-gather.3
  638.4 59.9 %all-reduce.10.cloned.1.call-done = (f32[1,256,1024]{2,1,0:T(8,128)}, f32[256,1024]{1,0:T(8,128)}) async-done(((f32[1,256,1024]{2,1,0:T(8,128)}, f32[256,1024]{1,0:T(8,128)}), (f32[1,256,1024]{2,1,0:T(8,128)}, f32[256,1024]{1,0:T(8,128)})) %all-reduce.10.cloned.1.call-update) | async-done | bytes 2097168 | tf_op jit(solution)/shard_map/psum | solution.py:145
  700.2 62.2 %all-reduce.4 = (f32[1024]{0:T(1024)}, f32[4,1024]{1,0:T(4,128)}, f32[4,256]{1,0:T(4,128)}, f32[16]{0:T(128)}, f32[16]{0:T(128)}, /*index=5*/f32[16]{0:T(128)}, f32[1024]{0:T(1024)}) all-reduce(f32[1024]{0:T(1024)S(1)} %get-tuple-element.317, f32[4,1024]{1,0:T(4,128)S(1)} %slice.219, ...), channel_id=1, replica_groups=mesh['fsdp'=4,'ctx'=4,'tp'=2] {'fsdp','ctx'}, use_global_device_ids=true, to_apply=%region_27.28 | all-reduce | flops 7216 | bytes 57728 | tf_op jit(solution)/shard_map/psum | solution.py:254
  762.5 2.8 fusion.55
  765.2 7.0 all_gather.60
  772.3 2.6 copy.228
  (303 shorter events, 84.4 us)
Async XLA Ops:
  7.2 59.4 %all-gather.13.cloned.1.call-start = ((), (), s32[]{:S(2)}) async-start(), calls=%async_computation.10 | async-start | bytes 2621440 | tf_op jit(solution)/shard_map/all_gather | solution.py:93
  7.9 96.3 %all-gather.25.cloned.1.call-start = ((), (), s32[]{:S(2)}) async-start(), calls=%async_computation.24 | async-start | bytes 2621440 | tf_op jit(solution)/shard_map/all_gather | solution.py:20
  23.0 6.3 copy-start.44
  26.0 26.7 %copy-start.2 = (bf16[1,256,1024]{2,1,0:T(8,128)(2,1)S(1)}, bf16[1,256,1024]{2,1,0:T(8,128)(2,1)}, u32[]{:S(2)}) copy-start(bf16[1,256,1024]{2,1,0:T(8,128)(2,1)} %param.26) | copy-start | bytes 1572868
  26.1 26.7 %copy-start.37 = (f32[1024]{0:T(1024)S(1)}, f32[1024]{0:T(1024)}, u32[]{:S(2)}) copy-start(f32[1024]{0:T(1024)} %param.27) | copy-start | bytes 12292
  27.6 25.6 %copy-start.33 = (f32[1,16,256]{1,2,0:T(8,128)}, f32[1,16,256]{1,2,0:T(8,128)S(1)}, u32[]{:S(2)}) copy-start(f32[1,16,256]{1,2,0:T(8,128)S(1)} %get-tuple-element.380) | copy-start | bytes 49156
  27.6 25.6 %copy-start.29 = (f32[1,16,256]{1,2,0:T(8,128)}, f32[1,16,256]{1,2,0:T(8,128)S(1)}, u32[]{:S(2)}) copy-start(f32[1,16,256]{1,2,0:T(8,128)S(1)} %get-tuple-element.381) | copy-start | bytes 49156
  29.2 24.0 %copy-start.24 = (f32[1,16,256]{1,2,0:T(8,128)}, f32[1,16,256]{1,2,0:T(8,128)S(1)}, u32[]{:S(2)}) copy-start(f32[1,16,256]{1,2,0:T(8,128)S(1)} %get-tuple-element.365) | copy-start | bytes 49156
  53.2 18.5 %copy-start.21 = (f32[1,256,256]{2,1,0:T(8,128)}, f32[1,256,256]{2,1,0:T(8,128)S(1)}, u32[]{:S(2)}) copy-start(f32[1,256,256]{2,1,0:T(8,128)S(1)} %convolution_bitcast_fusion.3) | copy-start | bytes 786436
  53.2 15.7 %copy-start.65 = (f32[16]{0:T(128)}, f32[16]{0:T(128)S(1)}, u32[]{:S(2)}) copy-start(f32[16]{0:T(128)S(1)} %get-tuple-element.374) | copy-start | bytes 196
  69.0 2.6 collective-permute-start
  77.2 29.0 %copy-start.7 = (f32[1,256,1024]{1,2,0:T(8,128)}, f32[1,256,1024]{1,2,0:T(8,128)S(1)}, u32[]{:S(2)}) copy-start(f32[1,256,1024]{1,2,0:T(8,128)S(1)} %copy.193) | copy-start | bytes 3145732
  80.2 9.8 %copy-start.35 = (f32[256,16]{1,0:T(8,128)S(1)}, f32[256,16]{1,0:T(8,128)}, u32[]{:S(2)}) copy-start(f32[256,16]{1,0:T(8,128)} %get-tuple-element.364) | copy-start | bytes 49156
  80.2 71.5 %all-gather.15.cloned.1.call-start = ((), (), s32[]{:S(2)}) async-start(), calls=%async_computation.11 | async-start | bytes 2621440 | tf_op jit(solution)/shard_map/all_gather | solution.py:92
  80.9 117.2 %all-gather.17.cloned.1.call-start = ((), (), s32[]{:S(2)}) async-start(), calls=%async_computation.12 | async-start | bytes 2621440 | tf_op jit(solution)/shard_map/all_gather | solution.py:96
  81.5 162.7 %all-gather.27.cloned.1.call-start = ((), (), s32[]{:S(2)}) async-start(), calls=%async_computation.25 | async-start | bytes 2621440 | tf_op jit(solution)/shard_map/all_gather | solution.py:20
  104.2 8.1 %copy-start.73 = (f32[4,1,16]{2,1,0:T(1,128)}, f32[4,1,16]{2,1,0:T(1,128)S(1)}, u32[]{:S(2)}) copy-start(f32[4,1,16]{2,1,0:T(1,128)S(1)} %get-tuple-element.621) | copy-start | bytes 772
  114.9 83.2 %copy-start.45 = (f32[1024]{0:T(1024)S(1)}, f32[1024]{0:T(1024)}, u32[]{:S(2)}) copy-start(f32[1024]{0:T(1024)} %param.37) | copy-start | bytes 12292
  155.4 69.0 %copy-start.5 = (f32[256,1024]{1,0:T(8,128)}, f32[256,1024]{1,0:T(8,128)S(1)}, u32[]{:S(2)}) copy-start(f32[256,1024]{1,0:T(8,128)S(1)} %get-tuple-element.363) | copy-start | bytes 3145732
  218.3 99.9 %reduce-scatter.15.cloned.1.call-start = ((), (), s32[]{:S(2)}) async-start(), calls=%async_computation.13 | async-start | bytes 5242880 | tf_op jit(solution)/shard_map/reduce_scatter | solution.py:234
  224.3 173.7 %reduce-scatter.29.cloned.1.call-start = ((), (), s32[]{:S(2)}) async-start(), calls=%async_computation.22 | async-start | bytes 5242880 | tf_op jit(solution)/shard_map/reduce_scatter | solution.py:238
  228.3 249.2 %reduce-scatter.19.cloned.1.call-start = ((), (), s32[]{:S(2)}) async-start(), calls=%async_computation.16 | async-start | bytes 5242880 | tf_op jit(solution)/shard_map/reduce_scatter | solution.py:235
  231.0 10.1 %copy-start.13 = (f32[256,1024]{0,1:T(8,128)S(1)}, f32[256,1024]{0,1:T(8,128)}, u32[]{:S(2)}) copy-start(f32[256,1024]{0,1:T(8,128)} %copy.208) | copy-start | bytes 3145732
  280.9 3.1 collective-permute-start.1
  289.5 210.4 %reduce-scatter.27.cloned.1.call-start = ((), (), s32[]{:S(2)}) async-start(), calls=%async_computation.21 | async-start | bytes 81920 | tf_op jit(solution)/shard_map/reduce_scatter | solution.py:237
  293.1 7.2 copy-start.11
  299.3 15.4 %copy-start.40 = (bf16[1,16,256]{1,2,0:T(8,128)(2,1)}, bf16[1,16,256]{1,2,0:T(8,128)(2,1)S(1)}, u32[]{:S(2)}) copy-start(bf16[1,16,256]{1,2,0:T(8,128)(2,1)S(1)} %get-tuple-element.358) | copy-start | bytes 24580
  300.3 227.8 %reduce-scatter.23.cloned.1.call-start = ((), (), s32[]{:S(2)}) async-start(), calls=%async_computation.19 | async-start | bytes 1310720 | tf_op jit(solution)/shard_map/reduce_scatter | solution.py:236
  314.8 239.6 %reduce-scatter.17.cloned.1.call-start = ((), (), s32[]{:S(2)}) async-start(), calls=%async_computation.14 | async-start | bytes 1310720 | tf_op jit(solution)/shard_map/reduce_scatter | solution.py:241
  318.3 263.3 %reduce-scatter.33.cloned.1.call-start = ((), (), s32[]{:S(2)}) async-start(), calls=%async_computation.27 | async-start | bytes 1310720
  400.5 77.1 %copy-start.6 = (f32[256,1024]{1,0:T(8,128)S(1)}, f32[256,1024]{1,0:T(8,128)}, u32[]{:S(2)}) copy-start(f32[256,1024]{1,0:T(8,128)} %copy-done.5) | copy-start | bytes 3145732
  400.5 208.7 %reduce-scatter.21.cloned.1.call-start = ((), (), s32[]{:S(2)}) async-start(), calls=%async_computation.17 | async-start | bytes 1310720 | tf_op jit(solution)/shard_map/reduce_scatter | solution.py:242
  477.5 154.1 %reduce-scatter.31.cloned.1.call-start = ((), (), s32[]{:S(2)}) async-start(), calls=%async_computation.26 | async-start | bytes 163840
  482.7 18.8 %copy-start.41 = (bf16[1,16,256]{1,2,0:T(8,128)(2,1)S(1)}, bf16[1,16,256]{1,2,0:T(8,128)(2,1)}, u32[]{:S(2)}) copy-start(bf16[1,16,256]{1,2,0:T(8,128)(2,1)} %copy-done.40) | copy-start | bytes 24580
  482.7 18.8 %copy-start.43 = (bf16[1024,16]{0,1:T(8,128)(2,1)S(1)}, bf16[1024,16]{0,1:T(8,128)(2,1)}, u32[]{:S(2)}) copy-start(bf16[1024,16]{0,1:T(8,128)(2,1)} %copy-done.42) | copy-start | bytes 98308
  501.5 196.8 %all-reduce.10.cloned.1.call-start = ((), (), s32[]{:S(2)}) async-start(), calls=%async_computation.28 | async-start | bytes 4194304 | tf_op jit(solution)/shard_map/psum | solution.py:145
  502.8 106.5 %copy-start.56 = (f32[1024]{0:T(1024)S(1)}, f32[1024]{0:T(1024)}, u32[]{:S(2)}) copy-start(f32[1024]{0:T(1024)} %get-tuple-element.355) | copy-start | bytes 12292
  502.8 106.7 %copy-start.49 = (f32[1,1280]{1,0:T(1,128)S(1)}, f32[1,1280]{1,0:T(1,128)}, u32[]{:S(2)}) copy-start(f32[1,1280]{1,0:T(1,128)} %copy-done.48) | copy-start | bytes 15364
  502.8 106.7 %copy-start.51 = (f32[1,1280]{1,0:T(1,128)S(1)}, f32[1,1280]{1,0:T(1,128)}, u32[]{:S(2)}) copy-start(f32[1,1280]{1,0:T(1,128)} %copy-done.50) | copy-start | bytes 15364
  502.8 106.7 %copy-start.53 = (f32[1,1280]{1,0:T(1,128)S(1)}, f32[1,1280]{1,0:T(1,128)}, u32[]{:S(2)}) copy-start(f32[1,1280]{1,0:T(1,128)} %copy-done.52) | copy-start | bytes 15364
  502.8 106.7 %copy-start.55 = (f32[1,1280]{1,0:T(1,128)S(1)}, f32[1,1280]{1,0:T(1,128)}, u32[]{:S(2)}) copy-start(f32[1,1280]{1,0:T(1,128)} %copy-done.54) | copy-start | bytes 15364
  502.8 195.5 %copy-start.27 = (bf16[1024,256]{1,0:T(8,128)(2,1)S(1)}, bf16[1024,256]{1,0:T(8,128)(2,1)}, u32[]{:S(2)}) copy-start(bf16[1024,256]{1,0:T(8,128)(2,1)} %copy-done.26) | copy-start | bytes 1572868
  502.8 262.4 %reduce-scatter.25.cloned.1.call-start = ((), (), s32[]{:S(2)}) async-start(), calls=%async_computation.20 | async-start | bytes 327680 | tf_op jit(solution)/shard_map/reduce_scatter | solution.py:243
  528.1 244.2 %all-gather.19.cloned.1.call-start = ((), (), s32[]{:S(2)}) async-start(), calls=%async_computation.15 | async-start | bytes 1310720 | tf_op jit(solution)/shard_map/all_gather | solution.py:248
  554.4 217.9 %all-gather.23.cloned.1.call-start = ((), (), s32[]{:S(2)}) async-start(), calls=%async_computation.23 | async-start | bytes 1310720 | tf_op jit(solution)/shard_map/all_gather | solution.py:252
  581.6 194.9 %all-gather.21.cloned.1.call-start = ((), (), s32[]{:S(2)}) async-start(), calls=%async_computation.18 | async-start | bytes 1310720 | tf_op jit(solution)/shard_map/all_gather | solution.py:249
  698.3 64.1 %copy-start.28 = (bf16[1,256,1024]{2,1,0:T(8,128)(2,1)S(1)}, bf16[1,256,1024]{2,1,0:T(8,128)(2,1)}, u32[]{:S(2)}) copy-start(bf16[1,256,1024]{2,1,0:T(8,128)(2,1)} %param.39) | copy-start | bytes 1572868
  698.3 64.1 %copy-start.70 = (f32[256]{0:T(256)S(1)}, f32[256]{0:T(256)}, u32[]{:S(2)}) copy-start(f32[256]{0:T(256)} %get-tuple-element.376) | copy-start | bytes 3076
  (50 other events, 141.1 us)
Sparse Core Ops, SparseCore 0:
  9.6 56.9 all-gather.12
  80.3 23.7 all-gather.24
  105.7 45.9 all-gather.14
  153.1 44.9 all-gather.16
  218.4 20.8 all-gather.26
  241.5 76.7 reduce-scatter.14
  320.6 77.2 reduce-scatter.28
  400.2 77.2 reduce-scatter.18
  480.4 19.4 reduce-scatter.26
  502.7 25.3 reduce-scatter.22
  530.8 23.5 reduce-scatter.16
  556.7 24.8 reduce-scatter.32
  584.3 24.8 reduce-scatter.20
  612.1 19.5 reduce-scatter.30
  635.2 63.0 all-reduce.9
  700.6 20.0 reduce-scatter.24
  722.2 16.9 all-gather.18
  740.6 16.7 all-gather.22
  759.1 17.4 all-gather.20
where the time goes:
time: 796 us; the launch traced here: 787 us
  waiting for transfers between devices  466 us (59%)
  blocking collectives  142 us (18%)
  matrix products  71.4 us (9%)
  local copies, waits for them, and re-layouts  50.8 us (6%)
  other arithmetic  36.6 us (5%)
  between operations  15.3 us (2%)
    reduce_scatter x1, waiting for transfers between devices, on_device(): lax.psum_scatter(weight_grads[4], 'fsdp', scatter_dimension=1, tiled=True)  79.6 us
    reduce_scatter x1, waiting for transfers between devices, on_device(): lax.psum_scatter(weight_grads[1], 'fsdp', scatter_dimension=0, tiled=True)  77 us
    psum x1, blocking collectives, on_device(): lax.psum((grad_input_gain, grad_taps[:, :inner_here], grad_bc_conv, grad_...  62.2 us
    psum x1, waiting for transfers between devices, on_device(): lax.psum(jnp.dot(normed_out, full_out, preferred_element_type=jnp.float32...  59.9 us
    unnamed x21, waiting for transfers between devices  51.5 us
    all_gather x1, waiting for transfers between devices, on_device(): lax.all_gather(out_proj, 'fsdp', axis=1, tiled=True)  37.8 us
    all_gather x1, waiting for transfers between devices, on_device(): lax.all_gather(gate_proj, 'fsdp', axis=0, tiled=True)  36.8 us
    reduce_scatter x1, waiting for transfers between devices, on_device(): lax.psum_scatter(sectioned[1], 'ctx', scatter_dimension=0, tiled=True)  27.6 us
  transfers between devices with their start and end apart: 21, of which 17 were waited for; matrix products, arithmetic and copies ran while one was open for 16% of the time, Pallas kernels for 0%

commit v1 on v0

--- a/solution.py
+++ b/solution.py
@@ -5,6 +5,24 @@
 
 EPSILON = 1e-05
 FINE = lax.Precision.HIGHEST
+
+
+def gather_around(shard, axis, dim):
+    ways, here, lap = (lax.axis_size(axis), lax.axis_index(axis), shard.shape[dim])
+    shape = [n * ways if d == dim else n for d, n in enumerate(shard.shape)]
+    full = lax.dynamic_update_slice_in_dim(
+        jnp.zeros(shape, shard.dtype), shard, here * lap, axis=dim
+    )
+    going_up = going_down = shard
+    for far in range(1, ways // 2 + 1):
+        going_up = lax.ppermute(going_up, axis, [(d, (d + 1) % ways) for d in range(ways)])
+        full = lax.dynamic_update_slice_in_dim(full, going_up, (here - far) % ways * lap, axis=dim)
+        if 2 * far < ways:
+            going_down = lax.ppermute(going_down, axis, [(d, (d - 1) % ways) for d in range(ways)])
+            full = lax.dynamic_update_slice_in_dim(
+                full, going_down, (here + far) % ways * lap, axis=dim
+            )
+    return full
 
 
 def from_behind(block, axis, distance):
@@ -91,7 +109,7 @@
     full_gate, full_x, full_bc, full_dt, full_out = (
         lax.all_gather(gate_proj, "fsdp", axis=0, tiled=True),
         lax.all_gather(x_proj, "fsdp", axis=0, tiled=True),
-        lax.all_gather(bc_proj, "fsdp", axis=0, tiled=True),
+        gather_around(bc_proj, "fsdp", 0),
         lax.all_gather(dt_proj, "fsdp", axis=0, tiled=True),
         lax.all_gather(out_proj, "fsdp", axis=1, tiled=True),
     )

time: 796 us -> 792 us (level)
  blocking collectives: 142 us -> 118 us
  waiting for transfers between devices: 466 us -> 479 us
    all_gather x1 -> x0, blocking collectives: 22.7 us -> none  [on_device(): lax.all_gather(bc_proj, 'fsdp', axis=0, tiled=True)]
    ppermute x0 -> x3, waiting for transfers between devices: none -> 9.59 us  [the longest x2 9.59 us: gather_around(): lax.ppermute(going_up, axis, [(d, (d + 1) % ways) for d in range(ways)])]
    unnamed x163 -> x153, local copies, waits for them, and re-layouts: 18.6 us -> 18.1 us
  transfers between devices with their start and end apart: 21 -> 24, of which waited for: 17 -> 17; matrix products, arithmetic and copies ran while one was open for 16% -> 16% of each run, Pallas kernels for 0% -> 0%
where the time goes in v1:
time: 792 us; the launch traced here: 782 us
  waiting for transfers between devices  479 us (60%)
  blocking collectives  118 us (15%)
  matrix products  71.2 us (9%)
  local copies, waits for them, and re-layouts  52.9 us (7%)
  other arithmetic  36 us (5%)
  between operations  15.4 us (2%)
  starting transfers between devices  9.64 us (1%)
    reduce_scatter x1, waiting for transfers between devices, on_device(): lax.psum_scatter(weight_grads[4], 'fsdp', scatter_dimension=1, tiled=True)  79.6 us
    reduce_scatter x1, waiting for transfers between devices, on_device(): lax.psum_scatter(weight_grads[1], 'fsdp', scatter_dimension=0, tiled=True)  77 us
    psum x1, blocking collectives, on_device(): lax.psum((grad_input_gain, grad_taps[:, :inner_here], grad_bc_conv, grad_...  62.2 us
    psum x1, waiting for transfers between devices, on_device(): lax.psum(jnp.dot(normed_out, full_out, preferred_element_type=jnp.float32...  59.9 us
    unnamed x21, waiting for transfers between devices  51.6 us
    all_gather x1, waiting for transfers between devices, on_device(): lax.all_gather(out_proj, 'fsdp', axis=1, tiled=True)  37.7 us
    all_gather x1, waiting for transfers between devices, on_device(): lax.all_gather(gate_proj, 'fsdp', axis=0, tiled=True)  36.8 us
    reduce_scatter x1, waiting for transfers between devices, on_device(): lax.psum_scatter(sectioned[1], 'ctx', scatter_dimension=0, tiled=True)  27.5 us
  transfers between devices with their start and end apart: 24, of which 17 were waited for; matrix products, arithmetic and copies ran while one was open for 16% of the time, Pallas kernels for 0%

profile of v1, /device:TPU:0, one launch (start us, length us, event | category | flops | bytes accessed | tf_op | source)
XLA Modules:
  0.0 782.2 jit_solution(17402102279306774143)
XLA Ops:
  8.0 3.1 collective-permute-start
  13.1 13.8 %all_gather.46 = bf16[1024,16]{0,1:T(8,128)(2,1)S(1)} all-gather(bf16[256,16]{0,1:T(8,128)(2,1)} %param.31), channel_id=1, replica_groups=mesh['fsdp'=4,'ctx'=4,'tp'=2] {'fsdp'}, dimensions={0}, use_global_device_ids=true | all-gather | bytes 40960 | tf_op jit(solution)/shard_map/all_gather | solution.py:113
  33.4 9.6 %collective-permute-done.2 = bf16[256,256]{1,0:T(8,128)(2,1)S(1)} collective-permute-done((bf16[256,256]{1,0:T(8,128)(2,1)S(1)}, bf16[256,256]{1,0:T(8,128)(2,1)S(1)}, u32[]{:S(2)}, u32[]{:S(2)}) %collective-permute-start.2) | collective-permute-done | bytes 131104 | tf_op jit(solution)/shard_map/ppermute | solution.py:18
  43.5 17.7 %all-gather.13.cloned.1.call-done = bf16[1024,1024]{1,0:T(8,128)(2,1)} async-done(((bf16[256,1024]{1,0:T(8,128)(2,1)}), bf16[1024,1024]{1,0:T(8,128)(2,1)}) %all-gather.13.cloned.1.call-update) | async-done | bytes 2097168 | tf_op jit(solution)/shard_map/all_gather | solution.py:111
  73.4 2.8 fusion.62
  79.0 6.2 all-gather
  86.4 2.6 copy.207
  91.7 8.0 %all-gather.25.cloned.1.call-done = f32[64,64,128]{2,1,0:T(8,128)} async-done(((f32[16,64,128]{2,1,0:T(8,128)}), f32[64,64,128]{2,1,0:T(8,128)}) %all-gather.25.cloned.1.call-update) | async-done | bytes 2097168 | tf_op jit(solution)/shard_map/all_gather | solution.py:38
  101.8 6.0 fusion.36
  107.8 2.6 copy.205
  110.4 36.8 %all-gather.15.cloned.1.call-done = bf16[1024,1024]{1,0:T(8,128)(2,1)} async-done(((bf16[256,1024]{1,0:T(8,128)(2,1)}), bf16[1024,1024]{1,0:T(8,128)(2,1)}) %all-gather.15.cloned.1.call-update) | async-done | bytes 2097168 | tf_op jit(solution)/shard_map/all_gather | solution.py:110
  147.2 3.7 multiply_reduce_fusion.8
  150.9 4.9 psum.91
  155.8 37.7 %all-gather.17.cloned.1.call-done = bf16[1024,1024]{1,0:T(8,128)(2,1)} async-done(((bf16[1024,256]{1,0:T(8,128)(2,1)}), bf16[1024,1024]{1,0:T(8,128)(2,1)}) %all-gather.17.cloned.1.call-update) | async-done | bytes 2097168 | tf_op jit(solution)/shard_map/all_gather | solution.py:114
  193.5 4.0 fusion.49
  197.6 5.5 psum.93
  203.1 2.9 fusion.59
  208.2 2.6 copy.208
  210.8 3.0 fusion.88
  217.0 2.8 fusion.121
  219.8 3.9 fusion.68
  223.8 2.6 copy.211
  226.5 8.6 %fusion.8 = (f32[16,256]{1,0:T(8,128)}, f32[16,256]{1,0:T(8,128)}, f32[16,256]{1,0:T(8,128)}, f32[256,256]{1,0:T(8,128)S(1)}) fusion(f32[16,256]{1,0:T(8,128)S(1)} %copy-done.50, f32[256,256]{1,0:T(8,128)} %fusion.92, f32[16,256]{1,0:T(8,128)} %bitcast_add_fusion.8, pred[256,256]{1,0:T(8,128)(4,1)} %iota_compare_fusion, f32[16,64,256]{2,1,0:T(8,128)} %bitcast.308, ...), kind=kOutput, calls=%fused_computation.20 | convolution fusion | flops 820957184 | bytes 2768896 | tf_op jit(solution)/shard_map/transpose(jvp(bhts,bshp->bthp))/dot_general | solution.py:67
  239.8 6.0 while.31
  248.3 4.9 fusion.30
  255.8 3.1 fusion.42
  258.9 2.6 multiply_reduce_fusion.5
  264.3 4.5 scatter-add.11
  268.8 2.6 slice_add_fusion.1
  271.4 4.4 scatter-add.14
  282.2 2.8 fusion.77
  296.9 12.9 %all-reduce.11 = (bf16[256,256]{1,0:T(8,128)(2,1)S(1)}, f32[4,256]{1,0:T(4,128)}) all-reduce(f32[256,256]{1,0:T(8,128)S(1)} %slice_bitcast_fusion, f32[4,256]{1,0:T(4,128)S(1)} %pad_maximum_fusion.2), channel_id=1, replica_groups=mesh['fsdp'=4,'ctx'=4,'tp'=2] {'tp'}, use_global_device_ids=true, to_apply=%region_24.25 | all-reduce | flops 66560 | bytes 401408 | tf_op jit(solution)/shard_map/psum | solution.py:217
  313.8 79.6 %reduce-scatter.29.cloned.1.call-done = f32[1024,256]{1,0:T(8,128)} async-done(((f32[1024,1024]{1,0:T(8,128)}), f32[1024,256]{1,0:T(8,128)}) %reduce-scatter.29.cloned.1.call-update) | async-done | bytes 1048592 | tf_op jit(solution)/shard_map/reduce_scatter | solution.py:256
  393.5 2.5 copy.245
  396.1 77.0 %reduce-scatter.19.cloned.1.call-done = f32[256,1024]{1,0:T(8,128)} async-done(((f32[1024,1024]{1,0:T(8,128)}), f32[256,1024]{1,0:T(8,128)}) %reduce-scatter.19.cloned.1.call-update) | async-done | bytes 1048592 | tf_op jit(solution)/shard_map/reduce_scatter | solution.py:253
  473.2 3.5 convolution_bitcast_fusion
  479.4 16.1 %reduce-scatter.27.cloned.1.call-done = f32[256,16]{0,1:T(8,128)} async-done(((f32[1024,16]{0,1:T(8,128)}), f32[256,16]{0,1:T(8,128)}) %reduce-scatter.27.cloned.1.call-update) | async-done | bytes 16400 | tf_op jit(solution)/shard_map/reduce_scatter | solution.py:255
  498.4 25.3 %reduce-scatter.23.cloned.1.call-done = f32[256,256]{1,0:T(8,128)} async-done(((f32[1024,256]{1,0:T(8,128)}), f32[256,256]{1,0:T(8,128)}) %reduce-scatter.23.cloned.1.call-update) | async-done | bytes 262160 | tf_op jit(solution)/shard_map/reduce_scatter | solution.py:254
  523.7 26.2 %reduce-scatter.17.cloned.1.call-done = f32[64,1024]{1,0:T(8,128)} async-done(((f32[256,1024]{1,0:T(8,128)}), f32[64,1024]{1,0:T(8,128)}) %reduce-scatter.17.cloned.1.call-update) | async-done | bytes 262160 | tf_op jit(solution)/shard_map/reduce_scatter | solution.py:259
  550.0 27.2 %reduce-scatter.33.cloned.1.call-done = f32[64,1024]{1,0:T(8,128)} async-done(((f32[256,1024]{1,0:T(8,128)}), f32[64,1024]{1,0:T(8,128)}) %reduce-scatter.33.cloned.1.call-update) | async-done | bytes 262160
  577.3 27.5 %reduce-scatter.21.cloned.1.call-done = f32[64,1024]{1,0:T(8,128)} async-done(((f32[256,1024]{1,0:T(8,128)}), f32[64,1024]{1,0:T(8,128)}) %reduce-scatter.21.cloned.1.call-update) | async-done | bytes 262160 | tf_op jit(solution)/shard_map/reduce_scatter | solution.py:260
  605.0 22.2 %reduce-scatter.31.cloned.1.call-done = f32[64,16]{1,0:T(8,128)} async-done(((f32[256,16]{1,0:T(8,128)}), f32[64,16]{1,0:T(8,128)}) %reduce-scatter.31.cloned.1.call-update) | async-done | bytes 4112
  628.1 5.2 all-gather.3
  634.0 59.9 %all-reduce.10.cloned.1.call-done = (f32[1,256,1024]{2,1,0:T(8,128)}, f32[256,1024]{1,0:T(8,128)}) async-done(((f32[1,256,1024]{2,1,0:T(8,128)}, f32[256,1024]{1,0:T(8,128)}), (f32[1,256,1024]{2,1,0:T(8,128)}, f32[256,1024]{1,0:T(8,128)})) %all-reduce.10.cloned.1.call-update) | async-done | bytes 2097168 | tf_op jit(solution)/shard_map/psum | solution.py:163
  695.8 62.2 %all-reduce.4 = (f32[1024]{0:T(1024)}, f32[4,1024]{1,0:T(4,128)}, f32[4,256]{1,0:T(4,128)}, f32[16]{0:T(128)}, f32[16]{0:T(128)}, /*index=5*/f32[16]{0:T(128)}, f32[1024]{0:T(1024)}) all-reduce(f32[1024]{0:T(1024)S(1)} %get-tuple-element.317, f32[4,1024]{1,0:T(4,128)S(1)} %slice.219, ...), channel_id=1, replica_groups=mesh['fsdp'=4,'ctx'=4,'tp'=2] {'fsdp','ctx'}, use_global_device_ids=true, to_apply=%region_27.28 | all-reduce | flops 7216 | bytes 57728 | tf_op jit(solution)/shard_map/psum | solution.py:272
  758.1 2.8 fusion.55
  760.9 7.1 all_gather.56
  767.9 2.6 copy.228
  (303 shorter events, 90.3 us)
Async XLA Ops:
  7.2 54.0 %all-gather.13.cloned.1.call-start = ((), (), s32[]{:S(2)}) async-start(), calls=%async_computation.10 | async-start | bytes 2621440 | tf_op jit(solution)/shard_map/all_gather | solution.py:111
  7.9 91.7 %all-gather.25.cloned.1.call-start = ((), (), s32[]{:S(2)}) async-start(), calls=%async_computation.24 | async-start | bytes 2621440 | tf_op jit(solution)/shard_map/all_gather | solution.py:38
  8.0 25.3 %collective-permute-start = (bf16[256,256]{1,0:T(8,128)(2,1)}, bf16[256,256]{1,0:T(8,128)(2,1)S(1)}, u32[]{:S(2)}, u32[]{:S(2)}) collective-permute-start(bf16[256,256]{1,0:T(8,128)(2,1)} %param.30), channel_id=1, source_target_pairs={{0,8},{8,16},{16,24},{24,0},{1,9},{9,17},{17,25},{25,1},{2,10},{10... | collective-permute-start | bytes 393224 | tf_op jit(solution)/shard_map/ppermute | solution.py:18
  11.0 22.4 %collective-permute-start.1 = (bf16[256,256]{1,0:T(8,128)(2,1)}, bf16[256,256]{1,0:T(8,128)(2,1)S(1)}, u32[]{:S(2)}, u32[]{:S(2)}) collective-permute-start(bf16[256,256]{1,0:T(8,128)(2,1)} %param.30), channel_id=1, source_target_pairs={{0,24},{8,0},{16,8},{24,16},{1,25},{9,1},{17,9},{25,17},{2,26},{10... | collective-permute-start | bytes 393224 | tf_op jit(solution)/shard_map/ppermute | solution.py:21
  32.4 10.6 %copy-start.58 = (f32[16,2]{0,1:T(2,128)}, f32[16,2]{0,1:T(2,128)S(1)}, u32[]{:S(2)}) copy-start(f32[16,2]{0,1:T(2,128)S(1)} %slice_bitcast_fusion.3) | copy-start | bytes 388
  32.4 10.7 %copy-start.2 = (bf16[1,256,1024]{2,1,0:T(8,128)(2,1)S(1)}, bf16[1,256,1024]{2,1,0:T(8,128)(2,1)}, u32[]{:S(2)}) copy-start(bf16[1,256,1024]{2,1,0:T(8,128)(2,1)} %param.26) | copy-start | bytes 1572868
  32.4 10.7 %copy-start.37 = (f32[1024]{0:T(1024)S(1)}, f32[1024]{0:T(1024)}, u32[]{:S(2)}) copy-start(f32[1024]{0:T(1024)} %param.27) | copy-start | bytes 12292
  32.5 11.0 %copy-start.24 = (f32[1,16,256]{1,2,0:T(8,128)}, f32[1,16,256]{1,2,0:T(8,128)S(1)}, u32[]{:S(2)}) copy-start(f32[1,16,256]{1,2,0:T(8,128)S(1)} %get-tuple-element.365) | copy-start | bytes 49156
  33.1 10.4 %copy-start.60 = (f32[16]{0:T(128)}, f32[16]{0:T(128)S(1)}, u32[]{:S(2)}) copy-start(f32[16]{0:T(128)S(1)} %get-tuple-element.374) | copy-start | bytes 196
  33.2 30.3 %copy-start.45 = (f32[4,1280]{1,0:T(4,128)}, f32[4,1280]{1,0:T(4,128)S(1)}, u32[]{:S(2)}) copy-start(f32[4,1280]{1,0:T(4,128)S(1)} %constant_dynamic-update-slice_fusion) | copy-start | bytes 61444
  33.3 9.7 %collective-permute-start.2 = (bf16[256,256]{1,0:T(8,128)(2,1)S(1)}, bf16[256,256]{1,0:T(8,128)(2,1)S(1)}, u32[]{:S(2)}, u32[]{:S(2)}) collective-permute-start(bf16[256,256]{1,0:T(8,128)(2,1)S(1)} %collective-permute-done), channel_id=1, source_target_pairs={{0,8},{8,16},{16,24},{24,0},{1,9},{9,17},{17,25},{25,1},{2,10},{10... | collective-permute-start | bytes 393224 | tf_op jit(solution)/shard_map/ppermute | solution.py:18
  43.1 20.5 %copy-start.26 = (bf16[1024,256]{1,0:T(8,128)(2,1)}, bf16[1024,256]{1,0:T(8,128)(2,1)S(1)}, u32[]{:S(2)}) copy-start(bf16[1024,256]{1,0:T(8,128)(2,1)S(1)} %constant_dynamic-update-slice_fusion.2) | copy-start | bytes 1572868
  43.5 24.3 %copy-start.21 = (f32[1,256,256]{2,1,0:T(8,128)}, f32[1,256,256]{2,1,0:T(8,128)S(1)}, u32[]{:S(2)}) copy-start(f32[1,256,256]{2,1,0:T(8,128)S(1)} %convolution_bitcast_fusion.3) | copy-start | bytes 786436
  63.6 3.4 collective-permute-start.3
  73.4 28.4 %copy-start.7 = (f32[1,256,1024]{1,2,0:T(8,128)}, f32[1,256,1024]{1,2,0:T(8,128)S(1)}, u32[]{:S(2)}) copy-start(f32[1,256,1024]{1,2,0:T(8,128)S(1)} %copy.193) | copy-start | bytes 3145732
  76.2 71.0 %all-gather.15.cloned.1.call-start = ((), (), s32[]{:S(2)}) async-start(), calls=%async_computation.11 | async-start | bytes 2621440 | tf_op jit(solution)/shard_map/all_gather | solution.py:110
  77.0 116.6 %all-gather.17.cloned.1.call-start = ((), (), s32[]{:S(2)}) async-start(), calls=%async_computation.12 | async-start | bytes 2621440 | tf_op jit(solution)/shard_map/all_gather | solution.py:114
  77.5 162.2 %all-gather.27.cloned.1.call-start = ((), (), s32[]{:S(2)}) async-start(), calls=%async_computation.25 | async-start | bytes 2621440 | tf_op jit(solution)/shard_map/all_gather | solution.py:38
  101.7 6.1 copy-start.20
  110.4 83.2 %copy-start.41 = (f32[1024]{0:T(1024)S(1)}, f32[1024]{0:T(1024)}, u32[]{:S(2)}) copy-start(f32[1024]{0:T(1024)} %param.37) | copy-start | bytes 12292
  150.9 69.0 %copy-start.5 = (f32[256,1024]{1,0:T(8,128)}, f32[256,1024]{1,0:T(8,128)S(1)}, u32[]{:S(2)}) copy-start(f32[256,1024]{1,0:T(8,128)S(1)} %get-tuple-element.363) | copy-start | bytes 3145732
  155.8 64.0 %copy-start.43 = (f32[1,256]{1,0:T(1,128)}, f32[1,256]{1,0:T(1,128)S(1)}, u32[]{:S(2)}) copy-start(f32[1,256]{1,0:T(1,128)S(1)} %add_rsqrt_fusion) | copy-start | bytes 3076
  213.8 99.9 %reduce-scatter.15.cloned.1.call-start = ((), (), s32[]{:S(2)}) async-start(), calls=%async_computation.13 | async-start | bytes 5242880 | tf_op jit(solution)/shard_map/reduce_scatter | solution.py:252
  219.8 173.7 %reduce-scatter.29.cloned.1.call-start = ((), (), s32[]{:S(2)}) async-start(), calls=%async_computation.22 | async-start | bytes 5242880 | tf_op jit(solution)/shard_map/reduce_scatter | solution.py:256
  223.8 249.3 %reduce-scatter.19.cloned.1.call-start = ((), (), s32[]{:S(2)}) async-start(), calls=%async_computation.16 | async-start | bytes 5242880 | tf_op jit(solution)/shard_map/reduce_scatter | solution.py:253
  226.5 10.1 %copy-start.13 = (f32[256,1024]{0,1:T(8,128)S(1)}, f32[256,1024]{0,1:T(8,128)}, u32[]{:S(2)}) copy-start(f32[256,1024]{0,1:T(8,128)} %copy.208) | copy-start | bytes 3145732
  276.5 3.1 collective-permute-start.4
  285.1 210.4 %reduce-scatter.27.cloned.1.call-start = ((), (), s32[]{:S(2)}) async-start(), calls=%async_computation.21 | async-start | bytes 81920 | tf_op jit(solution)/shard_map/reduce_scatter | solution.py:255
  288.3 5.9 copy-start.36
  288.3 5.9 copy-start.68
  295.8 227.8 %reduce-scatter.23.cloned.1.call-start = ((), (), s32[]{:S(2)}) async-start(), calls=%async_computation.19 | async-start | bytes 1310720 | tf_op jit(solution)/shard_map/reduce_scatter | solution.py:254
  311.2 238.6 %reduce-scatter.17.cloned.1.call-start = ((), (), s32[]{:S(2)}) async-start(), calls=%async_computation.14 | async-start | bytes 1310720 | tf_op jit(solution)/shard_map/reduce_scatter | solution.py:259
  313.8 263.4 %reduce-scatter.33.cloned.1.call-start = ((), (), s32[]{:S(2)}) async-start(), calls=%async_computation.27 | async-start | bytes 1310720
  396.0 77.1 %copy-start.6 = (f32[256,1024]{1,0:T(8,128)S(1)}, f32[256,1024]{1,0:T(8,128)}, u32[]{:S(2)}) copy-start(f32[256,1024]{1,0:T(8,128)} %copy-done.5) | copy-start | bytes 3145732
  396.0 77.2 %copy-start.42 = (f32[1024]{0:T(1024)S(1)}, f32[1024]{0:T(1024)}, u32[]{:S(2)}) copy-start(f32[1024]{0:T(1024)} %param.37) | copy-start | bytes 12292
  396.0 77.2 %copy-start.44 = (f32[1,256]{1,0:T(1,128)S(1)}, f32[1,256]{1,0:T(1,128)}, u32[]{:S(2)}) copy-start(f32[1,256]{1,0:T(1,128)} %copy-done.43) | copy-start | bytes 3076
  396.1 208.7 %reduce-scatter.21.cloned.1.call-start = ((), (), s32[]{:S(2)}) async-start(), calls=%async_computation.17 | async-start | bytes 1310720 | tf_op jit(solution)/shard_map/reduce_scatter | solution.py:260
  473.1 154.1 %reduce-scatter.31.cloned.1.call-start = ((), (), s32[]{:S(2)}) async-start(), calls=%async_computation.26 | async-start | bytes 163840
  497.0 196.9 %all-reduce.10.cloned.1.call-start = ((), (), s32[]{:S(2)}) async-start(), calls=%async_computation.28 | async-start | bytes 4194304 | tf_op jit(solution)/shard_map/psum | solution.py:163
  498.3 106.5 %copy-start.48 = (f32[1024]{0:T(1024)S(1)}, f32[1024]{0:T(1024)}, u32[]{:S(2)}) copy-start(f32[1024]{0:T(1024)} %get-tuple-element.355) | copy-start | bytes 12292
  498.3 195.6 %copy-start.27 = (bf16[1024,256]{1,0:T(8,128)(2,1)S(1)}, bf16[1024,256]{1,0:T(8,128)(2,1)}, u32[]{:S(2)}) copy-start(bf16[1024,256]{1,0:T(8,128)(2,1)} %copy-done.26) | copy-start | bytes 1572868
  498.3 195.6 %copy-start.34 = (bf16[256,256]{1,0:T(8,128)(2,1)S(1)}, bf16[256,256]{1,0:T(8,128)(2,1)}, u32[]{:S(2)}) copy-start(bf16[256,256]{1,0:T(8,128)(2,1)} %copy-done.33) | copy-start | bytes 393220
  498.3 262.6 %reduce-scatter.25.cloned.1.call-start = ((), (), s32[]{:S(2)}) async-start(), calls=%async_computation.20 | async-start | bytes 327680 | tf_op jit(solution)/shard_map/reduce_scatter | solution.py:261
  523.6 244.3 %all-gather.19.cloned.1.call-start = ((), (), s32[]{:S(2)}) async-start(), calls=%async_computation.15 | async-start | bytes 1310720 | tf_op jit(solution)/shard_map/all_gather | solution.py:266
  549.9 218.0 %all-gather.23.cloned.1.call-start = ((), (), s32[]{:S(2)}) async-start(), calls=%async_computation.23 | async-start | bytes 1310720 | tf_op jit(solution)/shard_map/all_gather | solution.py:270
  577.2 194.9 %all-gather.21.cloned.1.call-start = ((), (), s32[]{:S(2)}) async-start(), calls=%async_computation.18 | async-start | bytes 1310720 | tf_op jit(solution)/shard_map/all_gather | solution.py:267
  693.9 64.1 %copy-start.28 = (bf16[1,256,1024]{2,1,0:T(8,128)(2,1)S(1)}, bf16[1,256,1024]{2,1,0:T(8,128)(2,1)}, u32[]{:S(2)}) copy-start(bf16[1,256,1024]{2,1,0:T(8,128)(2,1)} %param.39) | copy-start | bytes 1572868
  693.9 64.1 %copy-start.65 = (f32[256]{0:T(256)S(1)}, f32[256]{0:T(256)}, u32[]{:S(2)}) copy-start(f32[256]{0:T(256)} %get-tuple-element.376) | copy-start | bytes 3076
  (48 other events, 114.8 us)
Sparse Core Ops, SparseCore 0:
  9.6 51.5 all-gather.12
  76.4 23.2 all-gather.24
  101.2 45.9 all-gather.14
  148.6 44.8 all-gather.16
  214.0 20.8 all-gather.26
  237.0 76.7 reduce-scatter.14
  316.2 77.2 reduce-scatter.28
  395.8 77.2 reduce-scatter.18
  476.0 19.4 reduce-scatter.26
  498.2 25.3 reduce-scatter.22
  526.3 23.5 reduce-scatter.16
  552.3 24.8 reduce-scatter.32
  579.9 24.8 reduce-scatter.20
  607.6 19.5 reduce-scatter.30
  630.7 63.0 all-reduce.9
  696.2 20.0 reduce-scatter.24
  717.8 16.9 all-gather.18
  736.2 16.7 all-gather.22
  754.7 17.4 all-gather.20
